TPU v7x, 32 devices: a whole 2x2x4 slice. The times are simulated.
32 devices in a mesh: seq: 8 (over z, core), dp: 4 (over y, x).
Axes of the slice: x: 2, y: 2, z: 4, core: 2. Of those that a mesh axis runs over, the one named last changes fastest.
Arguments:
- state: bfloat16 [4, 2048, 1024], P('dp', 'seq'), may hold values from -6 to 6
- embedded: bfloat16 [4, 2048, 1024], P('dp', 'seq'), may hold values from -6 to 6
- cotangent: bfloat16 [4, 2048, 1024], P('dp', 'seq'), may hold values from -6 to 6
- w_adapt: bfloat16 [2048, 1024], replicated, may hold values from -0.125 to 0.125
- w_qkv: bfloat16 [1024, 3072], replicated, may hold values from -0.25 to 0.25
- w_out: bfloat16 [1024, 1024], replicated, may hold values from -0.1875 to 0.1875
- w_gate: bfloat16 [1024, 2816], replicated, may hold values from -0.1875 to 0.1875
- w_up: bfloat16 [1024, 2816], replicated, may hold values from -0.1875 to 0.1875
- w_down: bfloat16 [2816, 1024], replicated, may hold values from -0.109375 to 0.109375
- gains: bfloat16 [4, 1024], replicated, may hold values from 0.5 to 1.5
Outputs:
- layer_out: bfloat16 [4, 2048, 1024], P('dp', 'seq')
- grad_state: float32 [4, 2048, 1024], P('dp', 'seq')
- grad_embedded: float32 [4, 2048, 1024], P('dp', 'seq')
- grad_adapt: float32 [2048, 1024], P(('seq', 'dp'))
- grad_qkv: float32 [1024, 3072], P(('seq', 'dp'))
- grad_out: float32 [1024, 1024], P(('seq', 'dp'))
- grad_gate: float32 [1024, 2816], P(('seq', 'dp'))
- grad_up: float32 [1024, 2816], P(('seq', 'dp'))
- grad_down: float32 [2816, 1024], P(('seq', 'dp'))
- grad_gains: float32 [4, 1024], P(None, ('seq', 'dp'))
All inputs are finite; a program needn't handle non-finite values.
Results may differ from a plain program's by a relative error of at most 0.025.
Values may be sent and summed in bfloat16 or wider, within the bound.
A program may use at most 256 MiB of HBM per device.

v0:
```python
import math

import jax
import jax.numpy as jnp
from jax import lax
from jax.sharding import PartitionSpec as P

HEADS = 8
HEAD_DIM = 128


norm_eps = 1e-06
rope_base = 50000.0
masked_score = -1e30


def passed_along(value, axis, steps):
    count = lax.axis_size(axis)
    first, last = (max(0, -steps), min(count, count - steps))
    return lax.ppermute(value, axis, [(source, source + steps) for source in range(first, last)])


def shifted(block, axis, distance):
    devices = range(lax.axis_size(axis))
    route = [((i - distance) % len(devices), i) for i in devices]
    return lax.ppermute(block, axis, route)


def mean_norm(values_in, gain_row):
    return (
        values_in
        * lax.rsqrt(jnp.mean(values_in * values_in, axis=-1, keepdims=True) + norm_eps)
        * gain_row
    )


def norm_back(values_in, gain_row, upstream):
    inverse = lax.rsqrt(jnp.mean(values_in * values_in, axis=-1, keepdims=True) + norm_eps)
    scaled = upstream * gain_row
    value_grad = inverse * scaled - values_in * (inverse * inverse * inverse) * jnp.mean(
        values_in * scaled, axis=-1, keepdims=True
    )
    gain_grad = jnp.sum(upstream * values_in * inverse, axis=0)
    return (value_grad, gain_grad)


def angle_tables(positions):
    half_dim = HEAD_DIM // 2
    freqs = jnp.exp(
        jnp.arange(half_dim, dtype=jnp.float32) * (-2.0 * math.log(rope_base) / HEAD_DIM)
    )
    angles = positions.astype(jnp.float32)[:, None] * freqs[None, :]
    return (jnp.cos(angles)[:, None, :], jnp.sin(angles)[:, None, :])


def rotate(heads_in, cos_table, sin_table):
    half_dim = heads_in.shape[-1] // 2
    lower_half = heads_in[..., :half_dim]
    upper_half = heads_in[..., half_dim:]
    return jnp.concatenate(
        [
            lower_half * cos_table - upper_half * sin_table,
            upper_half * cos_table + lower_half * sin_table,
        ],
        axis=-1,
    )


def left_product(left_side, right_side):
    return lax.dot_general(
        left_side, right_side, (((0,), (0,)), ((), ())), preferred_element_type=jnp.float32
    )


def right_product(left_side, right_side):
    return lax.dot_general(
        left_side, right_side, (((1,), (1,)), ((), ())), preferred_element_type=jnp.float32
    )


def tile_size_for(length):
    return math.gcd(length, 512)


def to_heads(flat):
    return flat.reshape(flat.shape[0], flat.shape[1], HEADS, HEAD_DIM)


def score_tiles(
    query_tile,
    upstream_tile,
    logsum_tile,
    delta_tile,
    query_spots,
    key_tile,
    value_tile,
    key_spots,
    score_scale,
):
    scores = (
        jnp.einsum("sqhd,skhd->sqhk", query_tile, key_tile, preferred_element_type=jnp.float32)
        * score_scale
    )
    allowed = (query_spots[:, None] >= key_spots[None, :])[None, :, None, :]
    probs_tile = jnp.where(allowed, jnp.exp(scores - logsum_tile[..., None]), 0.0)
    prob_grad = jnp.einsum(
        "sqhd,skhd->sqhk", upstream_tile, value_tile, preferred_element_type=jnp.float32
    )
    score_grad = (probs_tile * (prob_grad - delta_tile[..., None])).astype(jnp.bfloat16)
    return (probs_tile.astype(jnp.bfloat16), score_grad)


def local(state, embedded, cotangent, w_adapt, w_qkv, w_out, w_gate, w_up, w_down, gains):
    seq_count, row_count, model_width = state.shape
    token_count = seq_count * row_count
    score_scale = 1.0 / math.sqrt(HEAD_DIM)
    group_size = lax.axis_size("seq")
    my_index = lax.axis_index("seq")
    positions = my_index * row_count + jnp.arange(row_count, dtype=jnp.int32)
    cos_table, sin_table = angle_tables(positions)
    gain_rows = gains.astype(jnp.float32)
    joined = jnp.concatenate([state, embedded], axis=-1).reshape(token_count, 2 * model_width)
    resid = jnp.dot(joined, w_adapt, preferred_element_type=jnp.float32)
    normed = mean_norm(resid, gain_rows[0]).astype(jnp.bfloat16)
    packed = jnp.dot(normed, w_qkv, preferred_element_type=jnp.float32).reshape(
        seq_count, row_count, 3 * model_width
    )
    queries = rotate(to_heads(packed[..., :model_width]), cos_table, sin_table).astype(jnp.bfloat16)
    key_heads = rotate(
        to_heads(packed[..., model_width : 2 * model_width]), cos_table, sin_table
    ).astype(jnp.bfloat16)
    value_heads = to_heads(packed[..., 2 * model_width :]).astype(jnp.bfloat16)
    key_rows = key_heads.reshape(seq_count, row_count, model_width)
    value_rows = value_heads.reshape(seq_count, row_count, model_width)
    start_state = (
        jnp.full((seq_count, row_count, HEADS), masked_score, jnp.float32),
        jnp.zeros((seq_count, row_count, HEADS), jnp.float32),
        jnp.zeros((seq_count, row_count, HEADS, HEAD_DIM), jnp.float32),
    )
    key_piece = lax.all_gather(key_rows, "seq", axis=1, tiled=True)
    value_piece = lax.all_gather(value_rows, "seq", axis=1, tiled=True)
    span_len = key_piece.shape[1]
    tile = tile_size_for(span_len)

    def tile_turn(tile_index, inner_state):
        peak_old, sum_old, weighted = inner_state
        begin_at = tile_index * tile
        key_tile = to_heads(lax.dynamic_slice_in_dim(key_piece, begin_at, tile, 1))
        value_tile = to_heads(lax.dynamic_slice_in_dim(value_piece, begin_at, tile, 1))
        key_spots = begin_at + jnp.arange(tile, dtype=jnp.int32)
        scores = (
            jnp.einsum("sqhd,skhd->sqhk", queries, key_tile, preferred_element_type=jnp.float32)
            * score_scale
        )
        allowed = (positions[:, None] >= key_spots[None, :])[None, :, None, :]
        scores = jnp.where(allowed, scores, masked_score)
        peak_new = jnp.maximum(peak_old, jnp.max(scores, axis=-1))
        exp_tile = jnp.where(allowed, jnp.exp(scores - peak_new[..., None]), 0.0)
        factor = jnp.exp(peak_old - peak_new)
        sum_new = sum_old * factor + jnp.sum(exp_tile, axis=-1)
        weighted = weighted * factor[..., None] + jnp.einsum(
            "sqhk,skhd->sqhd",
            exp_tile.astype(jnp.bfloat16),
            value_tile,
            preferred_element_type=jnp.float32,
        )
        return (peak_new, sum_new, weighted)

    peak_all, sum_all, weighted = lax.fori_loop(0, span_len // tile, tile_turn, start_state)
    attended = weighted / sum_all[..., None]
    logsum = peak_all + jnp.log(sum_all)
    attended_low = attended.astype(jnp.bfloat16).reshape(token_count, model_width)
    branch = jnp.dot(attended_low, w_out, preferred_element_type=jnp.float32)
    middle = resid + mean_norm(branch, gain_rows[1])
    normed_mid = mean_norm(middle, gain_rows[2]).astype(jnp.bfloat16)
    gate_pre = jnp.dot(normed_mid, w_gate, preferred_element_type=jnp.float32)
    up_pre = jnp.dot(normed_mid, w_up, preferred_element_type=jnp.float32)
    sigmoid_gate = jax.nn.sigmoid(gate_pre)
    silu_gate = gate_pre * sigmoid_gate
    hidden = (silu_gate * up_pre).astype(jnp.bfloat16)
    down_out = jnp.dot(hidden, w_down, preferred_element_type=jnp.float32)
    layer_out = middle + mean_norm(down_out, gain_rows[3])
    out_grad = cotangent.astype(jnp.float32).reshape(token_count, model_width)
    down_grad, gain_grad3 = norm_back(down_out, gain_rows[3], out_grad)
    down_low = down_grad.astype(jnp.bfloat16)
    grad_down = left_product(hidden, down_low)
    hidden_grad = right_product(down_low, w_down)
    gate_low = (
        hidden_grad * up_pre * sigmoid_gate * (1.0 + gate_pre * (1.0 - sigmoid_gate))
    ).astype(jnp.bfloat16)
    up_low = (hidden_grad * silu_gate).astype(jnp.bfloat16)
    grad_gate = left_product(normed_mid, gate_low)
    grad_up = left_product(normed_mid, up_low)
    mid_norm_grad = right_product(gate_low, w_gate) + right_product(up_low, w_up)
    middle_part, gain_grad2 = norm_back(middle, gain_rows[2], mid_norm_grad)
    middle_grad = out_grad + middle_part
    branch_grad, gain_grad1 = norm_back(branch, gain_rows[1], middle_grad)
    branch_low = branch_grad.astype(jnp.bfloat16)
    grad_out = left_product(attended_low, branch_low)
    attended_grad = (
        right_product(branch_low, w_out)
        .astype(jnp.bfloat16)
        .reshape(seq_count, row_count, HEADS, HEAD_DIM)
    )
    row_delta = jnp.sum(attended_grad.astype(jnp.float32) * attended, axis=-1)
    zero_heads = jnp.zeros((seq_count, row_count, HEADS, HEAD_DIM), jnp.float32)

    def back_tile(key_now, value_now, owner_index, query_grad, key_grad, value_grad):
        key_tile = to_heads(key_now)
        value_tile = to_heads(value_now)
        key_spots = owner_index * row_count + jnp.arange(row_count, dtype=jnp.int32)
        probs_low, score_grad = score_tiles(
            queries,
            attended_grad,
            logsum,
            row_delta,
            positions,
            key_tile,
            value_tile,
            key_spots,
            score_scale,
        )
        value_grad = value_grad + jnp.einsum(
            "sqhk,sqhd->skhd", probs_low, attended_grad, preferred_element_type=jnp.float32
        )
        query_grad = query_grad + jnp.einsum(
            "sqhk,skhd->sqhd", score_grad, key_tile, preferred_element_type=jnp.float32
        )
        key_grad = key_grad + jnp.einsum(
            "sqhk,sqhd->skhd", score_grad, queries, preferred_element_type=jnp.float32
        )
        return (query_grad, key_grad, value_grad)

    def hop_turn(hop_index, running):
        key_now, value_now, key_grad, value_grad, query_grad = running
        owner_index = (my_index - hop_index + group_size) % group_size
        query_grad, key_grad, value_grad = back_tile(
            key_now, value_now, owner_index, query_grad, key_grad, value_grad
        )
        key_now, value_now = passed_along((key_now, value_now), "seq", 1)
        key_grad, value_grad = (
            shifted(key_grad.astype(jnp.bfloat16), "seq", 1).astype(key_grad.dtype),
            shifted(value_grad.astype(jnp.bfloat16), "seq", 1).astype(value_grad.dtype),
        )
        return (key_now, value_now, key_grad, value_grad, query_grad)

    key_now, value_now, key_grad, value_grad, query_grad = lax.fori_loop(
        0, group_size - 1, hop_turn, (key_rows, value_rows, zero_heads, zero_heads, zero_heads)
    )
    query_grad, key_grad, value_grad = back_tile(
        key_now, value_now, (my_index + 1) % group_size, query_grad, key_grad, value_grad
    )
    key_grad, value_grad = (
        shifted(key_grad.astype(jnp.bfloat16), "seq", 1).astype(key_grad.dtype),
        shifted(value_grad.astype(jnp.bfloat16), "seq", 1).astype(value_grad.dtype),
    )
    query_back = rotate(query_grad * score_scale, cos_table, -sin_table).reshape(
        token_count, model_width
    )
    key_back = rotate(key_grad * score_scale, cos_table, -sin_table).reshape(
        token_count, model_width
    )
    packed_low = jnp.concatenate(
        [query_back, key_back, value_grad.reshape(token_count, model_width)], axis=-1
    ).astype(jnp.bfloat16)
    grad_qkv = left_product(normed, packed_low)
    normed_grad = right_product(packed_low, w_qkv)
    resid_part, gain_grad0 = norm_back(resid, gain_rows[0], normed_grad)
    resid_low = (middle_grad + resid_part).astype(jnp.bfloat16)
    grad_adapt = left_product(joined, resid_low)
    joined_grad = right_product(resid_low, w_adapt).reshape(seq_count, row_count, 2 * model_width)
    grad_gains = jnp.stack([gain_grad0, gain_grad1, gain_grad2, gain_grad3])
    summed = (
        lax.psum_scatter(grad_adapt, ("seq", "dp"), scatter_dimension=0, tiled=True),
        lax.psum_scatter(grad_qkv, ("seq", "dp"), scatter_dimension=0, tiled=True),
        lax.psum_scatter(grad_out, ("seq", "dp"), scatter_dimension=0, tiled=True),
        lax.psum_scatter(grad_gate, ("seq", "dp"), scatter_dimension=0, tiled=True),
        lax.psum_scatter(grad_up, ("seq", "dp"), scatter_dimension=0, tiled=True),
        lax.psum_scatter(grad_down, ("seq", "dp"), scatter_dimension=0, tiled=True),
        lax.psum_scatter(grad_gains, ("seq", "dp"), scatter_dimension=1, tiled=True),
    )
    return (
        layer_out.reshape(seq_count, row_count, model_width).astype(jnp.bfloat16),
        joined_grad[..., :model_width],
        joined_grad[..., model_width:],
        summed[0],
        summed[1],
        summed[2],
        summed[3],
        summed[4],
        summed[5],
        summed[6],
    )


def solution(mesh):
    placed = (
        P("dp", "seq", None),
        P("dp", "seq", None),
        P("dp", "seq", None),
        P(),
        P(),
        P(),
        P(),
        P(),
        P(),
        P(),
    )
    return jax.shard_map(
        local,
        mesh=mesh,
        in_specs=placed,
        out_specs=(
            P("dp", "seq", None),
            P("dp", "seq", None),
            P("dp", "seq", None),
            P(("seq", "dp"), None),
            P(("seq", "dp"), None),
            P(("seq", "dp"), None),
            P(("seq", "dp"), None),
            P(("seq", "dp"), None),
            P(("seq", "dp"), None),
            P(None, ("seq", "dp")),
        ),
        check_vma=False,
    )
```

profile of v0, /device:TPU:0, one launch (start us, length us, event | category | flops | bytes accessed | tf_op | source)
XLA Modules:
  0.0 1814.2 jit_solution(18119067506652965319)
XLA Ops:
  8.7 4.0 multiply_reduce_fusion.10
  32.7 35.2 %all-gather.5.cloned.1.call-done = bf16[1,2048,1024]{2,1,0:T(8,128)(2,1)} async-done(((bf16[1,256,1024]{2,1,0:T(8,128)(2,1)}), bf16[1,2048,1024]{2,1,0:T(8,128)(2,1)}) %all-gather.5.cloned.1.call-update) | async-done | bytes 4194320 | tf_op jit(solution)/shard_map/all_gather | solution.py:141
  67.9 48.1 %all-gather.3.cloned.1.call-done = bf16[1,2048,1024]{1,2,0:T(8,128)(2,1)} async-done(((bf16[1,256,1024]{1,2,0:T(8,128)(2,1)}), bf16[1,2048,1024]{1,2,0:T(8,128)(2,1)}) %all-gather.3.cloned.1.call-update) | async-done | bytes 4194320 | tf_op jit(solution)/shard_map/all_gather | solution.py:140
  116.0 35.5 %while.42 = (s32[]{:T(128)}, f32[1,256,8]{1,2,0:T(8,128)S(1)}, f32[1,256,8]{1,2,0:T(8,128)S(1)}, f32[1,256,8,128]{1,3,2,0:T(8,128)}, bf16[1,2048,1024]{1,2,0:T(8...) while((s32[]{:T(128)}, f32[1,256,8]{1,2,0:T(8,128)S(1)}, ...), condition=%wide.region_4.5_spmd.clone, body=%wide.region_1.4_spmd.clone.sunk | while | flops 551432960 | bytes 36837656 | solution.py:169
  154.4 4.8 fusion.82
  159.2 3.5 multiply_convert_fusion.2
  166.3 5.6 multiply_convert_fusion
  181.1 207.4 %while.43 = (s32[]{:T(128)}, bf16[1,256,1024]{2,1,0:T(8,128)(2,1)}, bf16[1,256,1024]{2,1,0:T(8,128)(2,1)}, f32[1,256,8,128]{3,1,2,0:T(8,128)}, f32[1,256,8,128]{...) while((s32[]{:T(128)}, bf16[1,256,1024]{2,1,0:T(8,128)(2,1)}, ...), condition=%wide.region_13.14_spmd.clone, body=%wide.region_12.13_spmd.clone.sunk | while | flops 677446144 | bytes 44716592 | solution.py:247
  188.2 3.0 collective-permute-start
  191.1 2.8 collective-permute-start.1
  199.4 3.5 collective-permute-done.3
  210.5 5.1 collective-permute-start.2
  219.4 2.7 collective-permute-start
  222.1 3.0 collective-permute-start.1
  225.2 2.9 fusion.171
  237.7 9.1 collective-permute-start.2
  250.7 2.7 collective-permute-start
  253.4 3.0 collective-permute-start.1
  256.4 2.9 fusion.171
  268.9 9.1 collective-permute-start.2
  284.7 3.0 collective-permute-start.1
  287.7 2.9 fusion.171
  300.2 9.1 collective-permute-start.2
  315.9 3.0 collective-permute-start.1
  318.9 2.9 fusion.171
  331.5 9.1 collective-permute-start.2
  347.2 3.0 collective-permute-start.1
  350.2 2.9 fusion.171
  362.7 9.1 collective-permute-start.2
  375.7 2.7 collective-permute-start
  378.4 3.0 collective-permute-start.1
  381.4 2.9 fusion.171
  397.0 9.2 collective-permute-start.4
  412.5 5.7 collective-permute-done.5
  418.3 5.9 multiply_reduce_fusion.2
  431.0 4.5 fusion.63
  436.6 7.6 fusion.65
  445.7 5.9 fusion.86
  452.9 5.9 fusion.85
  460.4 6.0 fusion.87
  466.4 3.6 convolution_bitcast_fusion.4
  471.7 90.2 %reduce-scatter.22.cloned.1.call-done = f32[32,4]{1,0:T(8,128)} async-done(((f32[1024,4]{1,0:T(8,128)}), f32[32,4]{1,0:T(8,128)}) %reduce-scatter.22.cloned.1.call-update) | async-done | bytes 528
  563.2 139.1 %reduce-scatter.14.cloned.1.call-done = f32[32,1024]{1,0:T(8,128)} async-done(((f32[1024,1024]{1,0:T(8,128)}), f32[32,1024]{1,0:T(8,128)}) %reduce-scatter.14.cloned.1.call-update) | async-done | bytes 131088 | tf_op jit(solution)/shard_map/reduce_scatter | solution.py:276
  702.3 184.6 %reduce-scatter.10.cloned.1.call-done = f32[64,1024]{1,0:T(8,128)} async-done(((f32[2048,1024]{1,0:T(8,128)}), f32[64,1024]{1,0:T(8,128)}) %reduce-scatter.10.cloned.1.call-update) | async-done | bytes 262160 | tf_op jit(solution)/shard_map/reduce_scatter | solution.py:274
  886.9 163.9 %reduce-scatter.12.cloned.1.call-done = f32[32,3072]{1,0:T(8,128)} async-done(((f32[1024,3072]{1,0:T(8,128)}), f32[32,3072]{1,0:T(8,128)}) %reduce-scatter.12.cloned.1.call-update) | async-done | bytes 393232 | tf_op jit(solution)/shard_map/reduce_scatter | solution.py:275
  1050.8 250.7 %reduce-scatter.18.cloned.1.call-done = f32[32,2816]{1,0:T(8,128)} async-done(((f32[1024,2816]{1,0:T(8,128)}), f32[32,2816]{1,0:T(8,128)}) %reduce-scatter.18.cloned.1.call-update) | async-done | bytes 360464 | tf_op jit(solution)/shard_map/reduce_scatter | solution.py:278
  1301.5 252.8 %reduce-scatter.16.cloned.1.call-done = f32[32,2816]{1,0:T(8,128)} async-done(((f32[1024,2816]{1,0:T(8,128)}), f32[32,2816]{1,0:T(8,128)}) %reduce-scatter.16.cloned.1.call-update) | async-done | bytes 360464 | tf_op jit(solution)/shard_map/reduce_scatter | solution.py:277
  1554.3 253.0 %reduce-scatter.20.cloned.1.call-done = f32[88,1024]{1,0:T(8,128)} async-done(((f32[2816,1024]{1,0:T(8,128)}), f32[88,1024]{1,0:T(8,128)}) %reduce-scatter.20.cloned.1.call-update) | async-done | bytes 360464 | tf_op jit(solution)/shard_map/reduce_scatter | solution.py:279
  (450 shorter events, 204.6 us)
Async XLA Ops:
  7.2 145.7 %copy-start = (bf16[1024,1024]{1,0:T(8,128)(2,1)S(1)}, bf16[1024,1024]{1,0:T(8,128)(2,1)}, u32[]{:S(2)}) copy-start(bf16[1024,1024]{1,0:T(8,128)(2,1)} %param.19) | copy-start | bytes 6291460
  7.2 60.7 %all-gather.5.cloned.1.call-start = ((), (), s32[]{:S(2)}) async-start(), calls=%async_computation.8 | async-start | bytes 4718592 | tf_op jit(solution)/shard_map/all_gather | solution.py:141
  17.9 98.1 %all-gather.3.cloned.1.call-start = ((), (), s32[]{:S(2)}) async-start(), calls=%async_computation.7 | async-start | bytes 4718592 | tf_op jit(solution)/shard_map/all_gather | solution.py:140
  28.5 533.3 %reduce-scatter.22.cloned.1.call-start = ((), (), s32[]{:S(2)}) async-start(), calls=%async_computation.15 | async-start | bytes 540672
  186.6 10.7 collective-permute-start.2
  188.1 14.8 collective-permute-start.3
  188.2 16.8 collective-permute-start
  191.1 13.9 collective-permute-start.1
  210.5 17.5 collective-permute-start.2
  216.8 13.3 collective-permute-start.3
  219.4 12.8 collective-permute-start
  222.1 10.0 collective-permute-start.1
  235.3 11.6 copy-start.4
  237.7 21.6 %collective-permute-start.2 = (bf16[1,256,8,128]{3,1,2,0:T(8,128)(2,1)}, bf16[1,256,8,128]{3,1,2,0:T(8,128)(2,1)}, u32[]{:S(2)}, u32[]{:S(2)}) collective-permute-start(bf16[1,256,8,128]{3,1,2,0:T(8,128)(2,1)} %fusion.169), channel_id=1, source_target_pairs={{28,0},{0,4},{4,8},{8,12},{12,16},{16,20},{20,24},{24,28},{29,1},{... | collective-permute-start | bytes 1572872 | tf_op jit(solution)/shard_map/while/body/eval_jaxpr/ppermute | solution.py:26
  248.1 13.3 collective-permute-start.3
  250.7 12.8 collective-permute-start
  253.4 10.0 collective-permute-start.1
  266.5 11.6 copy-start.4
  268.9 21.6 %collective-permute-start.2 = (bf16[1,256,8,128]{3,1,2,0:T(8,128)(2,1)}, bf16[1,256,8,128]{3,1,2,0:T(8,128)(2,1)}, u32[]{:S(2)}, u32[]{:S(2)}) collective-permute-start(bf16[1,256,8,128]{3,1,2,0:T(8,128)(2,1)} %fusion.169), channel_id=1, source_target_pairs={{28,0},{0,4},{4,8},{8,12},{12,16},{16,20},{20,24},{24,28},{29,1},{... | collective-permute-start | bytes 1572872 | tf_op jit(solution)/shard_map/while/body/eval_jaxpr/ppermute | solution.py:26
  279.4 13.3 collective-permute-start.3
  281.9 12.8 collective-permute-start
  284.7 10.0 collective-permute-start.1
  297.8 11.6 copy-start.4
  300.2 21.6 %collective-permute-start.2 = (bf16[1,256,8,128]{3,1,2,0:T(8,128)(2,1)}, bf16[1,256,8,128]{3,1,2,0:T(8,128)(2,1)}, u32[]{:S(2)}, u32[]{:S(2)}) collective-permute-start(bf16[1,256,8,128]{3,1,2,0:T(8,128)(2,1)} %fusion.169), channel_id=1, source_target_pairs={{28,0},{0,4},{4,8},{8,12},{12,16},{16,20},{20,24},{24,28},{29,1},{... | collective-permute-start | bytes 1572872 | tf_op jit(solution)/shard_map/while/body/eval_jaxpr/ppermute | solution.py:26
  310.6 13.3 collective-permute-start.3
  313.2 12.8 collective-permute-start
  315.9 10.0 collective-permute-start.1
  329.0 11.6 copy-start.4
  331.5 21.6 %collective-permute-start.2 = (bf16[1,256,8,128]{3,1,2,0:T(8,128)(2,1)}, bf16[1,256,8,128]{3,1,2,0:T(8,128)(2,1)}, u32[]{:S(2)}, u32[]{:S(2)}) collective-permute-start(bf16[1,256,8,128]{3,1,2,0:T(8,128)(2,1)} %fusion.169), channel_id=1, source_target_pairs={{28,0},{0,4},{4,8},{8,12},{12,16},{16,20},{20,24},{24,28},{29,1},{... | collective-permute-start | bytes 1572872 | tf_op jit(solution)/shard_map/while/body/eval_jaxpr/ppermute | solution.py:26
  341.9 13.3 collective-permute-start.3
  344.5 12.8 collective-permute-start
  347.2 10.0 collective-permute-start.1
  360.3 11.6 copy-start.4
  362.7 21.6 %collective-permute-start.2 = (bf16[1,256,8,128]{3,1,2,0:T(8,128)(2,1)}, bf16[1,256,8,128]{3,1,2,0:T(8,128)(2,1)}, u32[]{:S(2)}, u32[]{:S(2)}) collective-permute-start(bf16[1,256,8,128]{3,1,2,0:T(8,128)(2,1)} %fusion.169), channel_id=1, source_target_pairs={{28,0},{0,4},{4,8},{8,12},{12,16},{16,20},{20,24},{24,28},{29,1},{... | collective-permute-start | bytes 1572872 | tf_op jit(solution)/shard_map/while/body/eval_jaxpr/ppermute | solution.py:26
  373.1 13.3 collective-permute-start.3
  375.7 12.8 collective-permute-start
  378.4 10.0 collective-permute-start.1
  397.0 13.1 copy-start.7
  397.0 13.6 collective-permute-start.4
  407.5 10.7 collective-permute-start.5
  412.0 12.1 copy-start.29
  425.2 277.1 %reduce-scatter.14.cloned.1.call-start = ((), (), s32[]{:S(2)}) async-start(), calls=%async_computation.11 | async-start | bytes 4325376 | tf_op jit(solution)/shard_map/reduce_scatter | solution.py:276
  428.3 458.6 %reduce-scatter.10.cloned.1.call-start = ((), (), s32[]{:S(2)}) async-start(), calls=%async_computation.9 | async-start | bytes 8650752 | tf_op jit(solution)/shard_map/reduce_scatter | solution.py:274
  435.6 615.2 %reduce-scatter.12.cloned.1.call-start = ((), (), s32[]{:S(2)}) async-start(), calls=%async_computation.10 | async-start | bytes 12976128 | tf_op jit(solution)/shard_map/reduce_scatter | solution.py:275
  444.2 857.3 %reduce-scatter.18.cloned.1.call-start = ((), (), s32[]{:S(2)}) async-start(), calls=%async_computation.13 | async-start | bytes 11894784 | tf_op jit(solution)/shard_map/reduce_scatter | solution.py:278
  451.6 1102.7 %reduce-scatter.16.cloned.1.call-start = ((), (), s32[]{:S(2)}) async-start(), calls=%async_computation.12 | async-start | bytes 11894784 | tf_op jit(solution)/shard_map/reduce_scatter | solution.py:277
  458.9 1348.3 %reduce-scatter.20.cloned.1.call-start = ((), (), s32[]{:S(2)}) async-start(), calls=%async_computation.14 | async-start | bytes 11894784 | tf_op jit(solution)/shard_map/reduce_scatter | solution.py:279
  466.4 1340.8 %copy-start.1 = (bf16[1024,1024]{1,0:T(8,128)(2,1)S(1)}, bf16[1024,1024]{1,0:T(8,128)(2,1)}, u32[]{:S(2)}) copy-start(bf16[1024,1024]{1,0:T(8,128)(2,1)} %param.19) | copy-start | bytes 6291460
  (81 other events, 239.9 us)
Sparse Core Ops, SparseCore 0:
  18.0 49.8 all-gather.4
  69.4 46.5 all-gather.2
  425.4 136.4 reduce-scatter.21
  564.7 137.5 reduce-scatter.13
  705.1 181.7 reduce-scatter.9
  894.4 156.3 reduce-scatter.11
  1053.7 247.7 reduce-scatter.17
  1304.4 249.8 reduce-scatter.15
  1557.2 250.0 reduce-scatter.19
where the time goes:
time: 1830 us; the launch traced here: 1810 us
  waiting for transfers between devices  1430 us (78%)
  matrix products  131 us (7%)
  starting transfers between devices  119 us (7%)
  local copies, waits for them, and re-layouts  71.7 us (4%)
  other arithmetic  47.9 us (3%)
    reduce_scatter x1, waiting for transfers between devices, local(): lax.psum_scatter(grad_down, ('seq', 'dp'), scatter_dimension=0, tiled=True)  253 us
    reduce_scatter x1, waiting for transfers between devices, local(): lax.psum_scatter(grad_gate, ('seq', 'dp'), scatter_dimension=0, tiled=True)  253 us
    reduce_scatter x1, waiting for transfers between devices, local(): lax.psum_scatter(grad_up, ('seq', 'dp'), scatter_dimension=0, tiled=True)  251 us
    reduce_scatter x1, waiting for transfers between devices, local(): lax.psum_scatter(grad_adapt, ('seq', 'dp'), scatter_dimension=0, tiled=True)  185 us
    reduce_scatter x1, waiting for transfers between devices, local(): lax.psum_scatter(grad_qkv, ('seq', 'dp'), scatter_dimension=0, tiled=True)  164 us
    reduce_scatter x1, waiting for transfers between devices, local(): lax.psum_scatter(grad_out, ('seq', 'dp'), scatter_dimension=0, tiled=True)  139 us
    unnamed x10, waiting for transfers between devices  90.3 us
    ppermute x16, starting transfers between devices, shifted(): return lax.ppermute(block, axis, route)  78.4 us
  transfers between devices with their start and end apart: 39, of which 12 were waited for; matrix products, arithmetic and copies ran while one was open for 6% of the time, Pallas kernels for 0%

commit v1 on v0

v1 whole, which is shorter than its diff:
```python
import functools
import math

import jax
import jax.numpy as jnp
import numpy as np
from jax import lax
from jax.experimental import pallas as pl
from jax.experimental.pallas import tpu as pltpu
from jax.sharding import PartitionSpec as P

HEADS = 8
HEAD_DIM = 128
norm_eps = 1e-06
rope_base = 50000.0
F32 = jnp.float32
BF16 = jnp.bfloat16
NEG = -1e30
SCORE_SCALE = 1.0 / math.sqrt(HEAD_DIM)
LOG2E = 1.0 / math.log(2.0)


def mean_norm(values_in, gain_row):
    return (
        values_in
        * lax.rsqrt(jnp.mean(values_in * values_in, axis=-1, keepdims=True) + norm_eps)
        * gain_row
    )


def norm_back(values_in, gain_row, upstream):
    inverse = lax.rsqrt(jnp.mean(values_in * values_in, axis=-1, keepdims=True) + norm_eps)
    scaled = upstream * gain_row
    value_grad = inverse * scaled - values_in * (inverse * inverse * inverse) * jnp.mean(
        values_in * scaled, axis=-1, keepdims=True
    )
    gain_grad = jnp.sum(upstream * values_in * inverse, axis=0)
    return (value_grad, gain_grad)


def angle_tables(length):
    half_dim = HEAD_DIM // 2
    freqs = np.exp(
        np.arange(half_dim, dtype=np.float32) * np.float32(-2.0 * math.log(rope_base) / HEAD_DIM)
    ).astype(np.float32)
    angles = np.arange(length, dtype=np.float32)[:, None] * freqs[None, :]
    return np.cos(angles).astype(np.float32), np.sin(angles).astype(np.float32)


def rotate(heads_in, cos_table, sin_table):
    half_dim = heads_in.shape[-1] // 2
    lower_half = heads_in[..., :half_dim]
    upper_half = heads_in[..., half_dim:]
    return jnp.concatenate(
        [
            lower_half * cos_table - upper_half * sin_table,
            upper_half * cos_table + lower_half * sin_table,
        ],
        axis=-1,
    )


def dot(a, b):
    return lax.dot_general(a, b, (((1,), (0,)), ((), ())), preferred_element_type=F32)


def dot_tn(a, b):
    return lax.dot_general(a, b, (((0,), (0,)), ((), ())), preferred_element_type=F32)


def dot_nt(a, b):
    return lax.dot_general(a, b, (((1,), (1,)), ((), ())), preferred_element_type=F32)


def span(low, high, body, unrolled):
    if unrolled:
        for i in range(low, high):
            body(i)
    else:
        lax.fori_loop(low, high, lambda i, c: (body(i), c)[1], 0)


def causal_fill(block, fill):
    kv = lax.broadcasted_iota(jnp.int32, block.shape, 0)
    q = lax.broadcasted_iota(jnp.int32, block.shape, 1)
    return jnp.where(q >= kv, block, fill)


def attention_kernel(x_ref, o_ref, ot_ref, ls_ref, vt_ref, s_ref):
    n, hp, _, rows, _ = x_ref.shape
    unrolled = n <= 8
    factor = SCORE_SCALE * LOG2E
    for h in range(hp):
        for j in range(n):
            vt_ref[j] = x_ref[j, h, 2].astype(F32).T.astype(BF16)

        def query_block(i):
            q = x_ref[i, h, 0]
            diag = causal_fill(dot_nt(x_ref[i, h, 1], q), NEG)

            def first(j, peak):
                s = dot_nt(x_ref[j, h, 1], q)
                s_ref[j] = s
                return jnp.maximum(peak, jnp.max(s, axis=0, keepdims=True))

            peak = jnp.max(diag, axis=0, keepdims=True)
            if unrolled:
                for j in range(i):
                    peak = first(j, peak)
            else:
                peak = lax.fori_loop(0, i, first, peak)
            shift = peak * factor
            p = jnp.exp2(diag * factor - shift)
            total = jnp.sum(p, axis=0, keepdims=True)
            acc = dot(vt_ref[i], p.astype(BF16))

            def second(j, state):
                total, acc = state
                p = jnp.exp2(s_ref[j] * factor - shift)
                return (
                    total + jnp.sum(p, axis=0, keepdims=True),
                    acc + dot(vt_ref[j], p.astype(BF16)),
                )

            state = (total, acc)
            if unrolled:
                for j in range(i):
                    state = second(j, state)
            else:
                state = lax.fori_loop(0, i, second, state)
            total, acc = state
            acc = acc / total
            ot_ref[i, h] = acc
            o_ref[i, h] = acc.T.astype(BF16)
            ls_ref[i, h] = shift + jnp.log2(total)

        span(0, n, query_block, unrolled)


def attention(x):
    n, hp, _, rows, dim = x.shape
    pairs = n * (n + 1) // 2 * rows * rows * hp
    return pl.pallas_call(
        attention_kernel,
        name="attention",
        out_shape=(
            jax.ShapeDtypeStruct((n, hp, rows, dim), BF16),
            jax.ShapeDtypeStruct((n, hp, dim, rows), F32),
            jax.ShapeDtypeStruct((n, hp, 1, rows), F32),
        ),
        scratch_shapes=[
            pltpu.VMEM((n, dim, rows), BF16),
            pltpu.VMEM((n, rows, rows), F32),
        ],
        compiler_params=pltpu.CompilerParams(vmem_limit_bytes=40 << 20),
        cost_estimate=pl.CostEstimate(
            flops=pairs * dim * 8, bytes_accessed=x.size * 4, transcendentals=pairs
        ),
    )(x)


def attention_back_kernel(
    x_ref, g_ref, ot_ref, ls_ref, cos_ref, sin_ref, out_ref, kt_ref, dqt_ref, delta_ref
):
    n, hp, _, rows, _ = x_ref.shape
    unrolled = n <= 8
    factor = SCORE_SCALE * LOG2E
    for h in range(hp):
        for j in range(n):
            kt_ref[j] = x_ref[j, h, 1].astype(F32).T.astype(BF16)
            delta_ref[j] = jnp.sum(
                g_ref[j, h].astype(F32).T * ot_ref[j, h], axis=0, keepdims=True
            )

        def unrotated(value, i):
            turned = pl.ds(i * rows, rows)
            cos, sin = cos_ref[turned], sin_ref[turned]
            return rotate(value * SCORE_SCALE, cos, -sin).astype(BF16)

        def pair(i, j, diagonal):
            q, g = x_ref[i, h, 0], g_ref[i, h]
            p = jnp.exp2(dot_nt(x_ref[j, h, 1], q) * factor - ls_ref[i, h])
            if diagonal:
                p = causal_fill(p, 0.0)
            dv = dot(p.astype(BF16), g)
            ds = (p * (dot_nt(x_ref[j, h, 2], g) - delta_ref[i])).astype(BF16)
            dk = dot(ds, q)
            dqt = dot(kt_ref[j], ds)
            return dv, dk, dqt

        def key_block(j):
            dv, dk, dqt = pair(j, j, True)
            if unrolled:
                dqt_ref[j] = dqt if j == 0 else dqt_ref[j] + dqt
            else:
                dqt_ref[j] = jnp.where(j == 0, 0.0, dqt_ref[j]) + dqt

            def step(i, state):
                dv, dk = state
                v, k, t = pair(i, j, False)
                if unrolled:
                    dqt_ref[i] = t if j == 0 else dqt_ref[i] + t
                else:
                    dqt_ref[i] = jnp.where(j == 0, 0.0, dqt_ref[i]) + t
                return dv + v, dk + k

            state = (dv, dk)
            if unrolled:
                for i in range(j + 1, n):
                    state = step(i, state)
            else:
                state = lax.fori_loop(j + 1, n, step, state)
            dv, dk = state
            out_ref[j, h, 0] = unrotated(dqt_ref[j].T, j)
            out_ref[j, h, 1] = unrotated(dk, j)
            out_ref[j, h, 2] = dv.astype(BF16)

        span(0, n, key_block, unrolled)


def attention_back(x, g, ot, ls, cos, sin):
    n, hp, _, rows, dim = x.shape
    pairs = n * (n + 1) // 2 * rows * rows * hp
    return pl.pallas_call(
        attention_back_kernel,
        name="attention_back",
        out_shape=jax.ShapeDtypeStruct(x.shape, BF16),
        scratch_shapes=[
            pltpu.VMEM((n, dim, rows), BF16),
            pltpu.VMEM((n, dim, rows), F32),
            pltpu.VMEM((n, 1, rows), F32),
        ],
        compiler_params=pltpu.CompilerParams(vmem_limit_bytes=40 << 20),
        cost_estimate=pl.CostEstimate(
            flops=pairs * dim * 20, bytes_accessed=x.size * 6, transcendentals=pairs
        ),
    )(x, g, ot, ls, cos, sin)


def xor_permute(value, axis, mask):
    return lax.ppermute(value, axis, [(i, i ^ mask) for i in range(lax.axis_size(axis))])


def quadrants(left):
    n, parts = lax.axis_size("seq"), lax.axis_size("dp")
    tokens, rows = left.shape
    shard = rows // (n * parts)
    split = left.reshape(tokens, n, parts, shard).transpose(2, 0, 1, 3)
    split = split.reshape(parts, tokens, n * shard)
    me = lax.axis_index("dp")
    return jnp.concatenate(
        [lax.dynamic_index_in_dim(split, me ^ m, 0, keepdims=True) for m in range(parts)]
    )


def other_core(left, right):
    core = lax.axis_index("seq") % 2
    half = right.shape[1] // 2
    mine = lax.dynamic_slice_in_dim(right, core * half, half, 1)
    theirs = lax.dynamic_slice_in_dim(right, (1 - core) * half, half, 1)
    left_in = xor_permute(left, "seq", 1)
    right_in = xor_permute(theirs, "seq", 1)
    return jnp.concatenate([left, left_in], axis=1), jnp.concatenate([mine, right_in], axis=0)


def scattered_sum(left, right, bits):
    n, parts = lax.axis_size("seq"), lax.axis_size("dp")
    cols = right.shape[1]
    left, right = other_core(quadrants(left), right)
    got = {}
    masks = list(range(parts))
    for bit in bits:
        outgoing = [m for m in masks if m >> bit & 1]
        masks = [m for m in masks if not m >> bit & 1]
        blocks = []
        for m in outgoing:
            block = dot_tn(left[m], right)
            for more in got.get(m, ()):
                block = block + more.astype(F32)
            blocks.append(block.astype(BF16))
        incoming = xor_permute(jnp.stack(blocks), "dp", 1 << bit)
        for k, m in enumerate(outgoing):
            got.setdefault(m ^ (1 << bit), []).append(incoming[k])
    block = dot_tn(left[0], right)
    for more in got.get(0, ()):
        block = block + more.astype(F32)
    shard = block.shape[0] // n
    block = block.astype(BF16).reshape(n, shard, cols // 2)
    block = lax.all_to_all(block, "seq", 0, 0)
    block = jnp.sum(block.reshape(n // 2, 2, shard, cols // 2).astype(F32), axis=0)
    return block.transpose(1, 0, 2).reshape(shard, cols)


def local(state, embedded, cotangent, w_adapt, w_qkv, w_out, w_gate, w_up, w_down, gains):
    seq_count, rows, width = state.shape
    n, parts = lax.axis_size("seq"), lax.axis_size("dp")
    tokens = seq_count * rows
    me = lax.axis_index("seq")
    bits = list(range(parts.bit_length() - 1))
    copies = max(1, n // HEADS)
    held = max(1, HEADS // n)
    owners = n // copies
    cos_np, sin_np = angle_tables(n * rows)
    cos_all, sin_all = jnp.asarray(cos_np), jnp.asarray(sin_np)
    cos = lax.dynamic_slice_in_dim(cos_all, me * rows, rows, 0)[:, None, :]
    sin = lax.dynamic_slice_in_dim(sin_all, me * rows, rows, 0)[:, None, :]
    gain_rows = gains.astype(F32)
    state, embedded = state.reshape(tokens, width), embedded.reshape(tokens, width)

    def to_heads(flat):
        return flat.reshape(tokens, HEADS, HEAD_DIM)

    def to_owner(parts_in):
        sent = jnp.stack(parts_in).reshape(len(parts_in), tokens, owners, held, HEAD_DIM)
        sent = sent.transpose(2, 3, 0, 1, 4)
        if copies > 1:
            sent = jnp.repeat(sent, copies, axis=0)
        return lax.all_to_all(sent, "seq", 0, 0)

    def from_owner(value):
        back = lax.all_to_all(value, "seq", 0, 0)[::copies]
        back = back.reshape(HEADS, -1, tokens, HEAD_DIM)
        return back.transpose(2, 1, 0, 3).reshape(tokens, -1)

    resid = dot(state, w_adapt[:width]) + dot(embedded, w_adapt[width:])
    normed = mean_norm(resid, gain_rows[0]).astype(BF16)
    packed = dot(normed, w_qkv)
    queries = rotate(to_heads(packed[:, :width]), cos, sin).astype(BF16)
    keys = rotate(to_heads(packed[:, width : 2 * width]), cos, sin).astype(BF16)
    values = to_heads(packed[:, 2 * width :]).astype(BF16)
    qkv = to_owner((queries, keys, values))
    attended, attended_t, logsum = attention(qkv)
    attended = from_owner(attended[:, :, None])
    branch = dot(attended, w_out)
    middle = resid + mean_norm(branch, gain_rows[1])
    normed_mid = mean_norm(middle, gain_rows[2]).astype(BF16)
    gate_pre = dot(normed_mid, w_gate)
    up_pre = dot(normed_mid, w_up)
    sigmoid_gate = jax.nn.sigmoid(gate_pre)
    silu_gate = gate_pre * sigmoid_gate
    hidden = (silu_gate * up_pre).astype(BF16)
    down_out = dot(hidden, w_down)
    layer_out = middle + mean_norm(down_out, gain_rows[3])
    out_grad = cotangent.astype(F32).reshape(tokens, width)
    down_grad, gain_grad3 = norm_back(down_out, gain_rows[3], out_grad)
    down_low = down_grad.astype(BF16)
    hidden_grad = dot_nt(down_low, w_down)
    gate_low = (
        hidden_grad * up_pre * sigmoid_gate * (1.0 + gate_pre * (1.0 - sigmoid_gate))
    ).astype(BF16)
    up_low = (hidden_grad * silu_gate).astype(BF16)
    mid_norm_grad = dot_nt(gate_low, w_gate) + dot_nt(up_low, w_up)
    middle_part, gain_grad2 = norm_back(middle, gain_rows[2], mid_norm_grad)
    middle_grad = out_grad + middle_part
    branch_grad, gain_grad1 = norm_back(branch, gain_rows[1], middle_grad)
    branch_low = branch_grad.astype(BF16)
    attended_grad = dot_nt(branch_low, w_out).astype(BF16)
    upstream = to_owner((to_heads(attended_grad),))[:, :, 0]
    packed_grad = attention_back(qkv, upstream, attended_t, logsum, cos_all, sin_all)
    packed_low = from_owner(packed_grad)
    normed_grad = dot_nt(packed_low, w_qkv)
    resid_part, gain_grad0 = norm_back(resid, gain_rows[0], normed_grad)
    resid_low = (middle_grad + resid_part).astype(BF16)
    grad_state = dot_nt(resid_low, w_adapt[:width])
    grad_embedded = dot_nt(resid_low, w_adapt[width:])
    flipped = bits[::-1]
    joined = jnp.concatenate([state, embedded], axis=-1)
    grad_down = scattered_sum(hidden, down_low, bits)
    grad_gate = scattered_sum(normed_mid, gate_low, flipped)
    grad_up = scattered_sum(normed_mid, up_low, bits)
    grad_out = scattered_sum(attended, branch_low, flipped)
    grad_qkv = scattered_sum(normed, packed_low, flipped)
    grad_adapt = scattered_sum(joined, resid_low, bits)
    grad_gains = jnp.stack([gain_grad0, gain_grad1, gain_grad2, gain_grad3])
    grad_gains = lax.psum_scatter(grad_gains, ("seq", "dp"), scatter_dimension=1, tiled=True)
    shape = (seq_count, rows, width)
    return (
        layer_out.reshape(shape).astype(BF16),
        grad_state.reshape(shape),
        grad_embedded.reshape(shape),
        grad_adapt,
        grad_qkv,
        grad_out,
        grad_gate,
        grad_up,
        grad_down,
        grad_gains,
    )


def solution(mesh):
    tokens = P("dp", "seq", None)
    rows = P(("seq", "dp"), None)
    return jax.shard_map(
        local,
        mesh=mesh,
        in_specs=(tokens,) * 3 + (P(),) * 7,
        out_specs=(tokens,) * 3 + (rows,) * 6 + (P(None, ("seq", "dp")),),
        check_vma=False,
    )
```

time: 1830 us -> 568 us (0.31)
  waiting for transfers between devices: 1430 us -> 239 us
  starting transfers between devices: 119 us -> 58.7 us
  blocking collectives: 0 us -> 44 us
  matrix products: 131 us -> 92.5 us
  other arithmetic: 47.9 us -> 29.3 us
    reduce_scatter x6 -> x0, waiting for transfers between devices: 1240 us -> none  [the longest x1 253 us: local(): lax.psum_scatter(grad_down, ('seq', 'dp'), scatter_dimension=0, tiled=True)]
    ppermute x30 -> x23, starting transfers between devices: 118 us -> 19.5 us  [xor_permute(): lax.ppermute(value, axis, [(i, i ^ mask) for i in range(lax.axis_size(axi...]
    all_gather x2 -> x0, waiting for transfers between devices: 83.3 us -> none  [the longest x1 48.1 us: local(): key_piece = lax.all_gather(key_rows, 'seq', axis=1, tiled=True)]
    ppermute x30 -> x23, waiting for transfers between devices: 10.2 us -> 81.9 us  [xor_permute(): lax.ppermute(value, axis, [(i, i ^ mask) for i in range(lax.axis_size(axi...]
    all_to_all x0 -> x1, blocking collectives: none -> 44 us  [to_owner(): return lax.all_to_all(sent, 'seq', 0, 0)]
    unnamed x10 -> x2, waiting for transfers between devices: 90.3 us -> 130 us
    all_to_all x0 -> x9, starting transfers between devices: none -> 39.2 us  [the longest x6 25.1 us: scattered_sum(): block = lax.all_to_all(block, 'seq', 0, 0)]
    dot_general x66 -> x38, matrix products: 131 us -> 92.5 us  [the longest x24 42.8 us: dot_tn(): lax.dot_general(a, b, (((0,), (0,)), ((), ())), preferred_element_type=F32)]
  transfers between devices with their start and end apart: 39 -> 33, of which waited for: 12 -> 14; matrix products, arithmetic and copies ran while one was open for 6% -> 25% of each run, Pallas kernels for 0% -> 2%
where the time goes in v1:
time: 568 us; the launch traced here: 558 us
  waiting for transfers between devices  239 us (42%)
  matrix products  92.5 us (16%)
  local copies, waits for them, and re-layouts  62.1 us (11%)
  starting transfers between devices  58.7 us (10%)
  blocking collectives  44 us (8%)
  other arithmetic  29.3 us (5%)
  Pallas kernels  16.2 us (3%)
  between operations  15.9 us (3%)
    unnamed x2, waiting for transfers between devices  130 us
    ppermute x23, waiting for transfers between devices, xor_permute(): lax.ppermute(value, axis, [(i, i ^ mask) for i in range(lax.axis_size(axi...  81.9 us
    all_to_all x1, blocking collectives, to_owner(): return lax.all_to_all(sent, 'seq', 0, 0)  44 us
    dot_general x24, matrix products, dot_tn(): lax.dot_general(a, b, (((0,), (0,)), ((), ())), preferred_element_type=F32)  42.8 us
    unnamed x210, local copies, waits for them, and re-layouts  28.1 us
    all_to_all x6, waiting for transfers between devices, scattered_sum(): block = lax.all_to_all(block, 'seq', 0, 0)  26.7 us
    dot_general x7, matrix products, dot(): lax.dot_general(a, b, (((1,), (0,)), ((), ())), preferred_element_type=F32)  25.8 us
    all_to_all x6, starting transfers between devices, scattered_sum(): block = lax.all_to_all(block, 'seq', 0, 0)  25.1 us
  transfers between devices with their start and end apart: 33, of which 14 were waited for; matrix products, arithmetic and copies ran while one was open for 25% of the time, Pallas kernels for 2%

profile of v1, /device:TPU:0, one launch (start us, length us, event | category | flops | bytes accessed | tf_op | source)
XLA Modules:
  0.0 558.0 jit_solution(15883049755822930192)
XLA Ops:
  8.1 2.5 fusion.21
  10.6 2.6 multiply_reduce_fusion.9
  22.0 2.4 copy.108
  24.4 2.4 copy.107
  29.4 2.4 copy.109
  31.9 2.3 copy.110
  35.1 2.8 fusion.61
  38.7 44.0 %all_to_all.50.x_ref = bf16[8,1,3,256,128]{4,3,2,1,0:T(8,128)(2,1)S(1)} all-to-all(bf16[8,1,3,256,128]{4,3,2,1,0:T(8,128)(2,1)S(1)} %maximum_bitcast_fusion), channel_id=1, replica_groups=mesh['seq'=8,'dp'=4] {'seq'}, dimensions={0} | all-to-all | bytes 3145728 | tf_op jit(solution)/shard_map/all_to_all | solution.py:318
  82.6 5.6 %attention.1 = (bf16[8,1,256,128]{3,2,1,0:T(8,128)(2,1)}, f32[8,1,128,256]{3,2,1,0:T(8,128)S(1)}, f32[8,1,1,256]{3,2,1,0:T(1,128)S(1)}) custom-call(bf16[8,1,3,256,128]{4,3,2,1,0:T(8,128)(2,1)S(1)} %all_to_all.50.x_ref), custom_call_target="tpu_custom_call" | custom-call | flops 2415919104 | bytes 3145728 | tf_op jit(solution)/shard_map/attention/pallas_call | solution.py:143
  89.2 4.4 all-to-all-start.1
  118.4 4.5 fusion.73
  122.9 7.6 %multiply_convert_fusion.2 = (bf16[256,2816]{1,0:T(8,128)(2,1)}, f32[256,2816]{1,0:T(8,128)}) fusion(f32[256,2816]{1,0:T(8,128)S(1)} %fusion.73, bf16[256,1024]{1,0:T(8,128)(2,1)S(1)} %copy-done.46, bf16[1024,2816]{1,0:T(8,128)(2,1)} %param.19), kind=kOutput, calls=%fused_computation.3 | convolution fusion | flops 1480720384 | bytes 13500416 | tf_op jit(solution)/shard_map/dot_general | solution.py:64
  130.4 2.9 copy.102
  133.4 5.0 multiply_reduce_fusion.6
  140.8 6.0 %multiply_convert_fusion = (bf16[256,2816]{1,0:T(8,128)(2,1)S(1)}, bf16[256,2816]{1,0:T(8,128)(2,1)S(1)}) fusion(f32[256,2816]{1,0:T(8,128)S(1)} %copy-done.95, f32[256,2816]{1,0:T(8,128)S(1)} %copy-done.96, bf16[256,1024]{1,0:T(8,128)(2,1)S(1)} %get-tuple-element.45, bf16[2816,1024]{1,0:T(8,128)(2,1)} %param.20), kind=kOutput, calls=%fused_computation.1 | convolution fusion | flops 1485766656 | bytes 14942208 | tf_op jit(solution)/shard_map/dot_general | solution.py:72
  155.9 4.7 all-to-all-start.2
  178.6 10.5 %attention_back.1 = bf16[8,1,3,256,128]{4,3,2,1,0:T(8,128)(2,1)} custom-call(bf16[8,1,3,256,128]{4,3,2,1,0:T(8,128)(2,1)S(1)} %copy-done.3, bf16[8,1,256,128]{3,2,1,0:T(8,128)(2,1)S(1)} %bitcast.324, f32[8,1,128,256]{3,2,1,0:T(8,128)S(1)} %copy-done.7, f32[8,1,1,256]{3,2,1,0:T(1,128)S(1)} %get-tuple-element.15.ls_ref, f32[2048,64]{1,0:T(8,128)S(1)} %copy-done.5, ...), custom_call_target="tpu_custom_call" | custom-call | flops 6039797760 | bytes 4718592 | tf_op jit(solution)/shard_map/attention_back/pallas_call | solution.py:224
  189.1 4.9 all-to-all-start.3
  207.8 2.8 pad_maximum_fusion.1
  210.6 17.9 %collective-permute-done.14 = bf16[2,256,1408]{2,1,0:T(8,128)(2,1)} collective-permute-done((bf16[2,256,1408]{2,1,0:T(8,128)(2,1)}, bf16[2,256,1408]{2,1,0:T(8,128)(2,1)}, u32[]{:S(2)}, u32[]{:S(2)}) %collective-permute-start.14) | collective-permute-done | bytes 1441824 | tf_op jit(solution)/shard_map/ppermute | solution.py:241
  231.7 35.6 %collective-permute-done.11 = bf16[1,256,512]{2,1,0:T(8,128)(2,1)S(1)} collective-permute-done((bf16[1,256,512]{2,1,0:T(8,128)(2,1)S(1)}, bf16[1,256,512]{2,1,0:T(8,128)(2,1)S(1)}, u32[]{:S(2)}, u32[]{:S(2)}) %collective-permute-start.11) | collective-permute-done | bytes 262176 | tf_op jit(solution)/shard_map/ppermute | solution.py:241
  269.4 2.6 fusion.17
  273.5 2.8 fusion.44
  276.9 5.2 collective-permute-done.15
  282.1 2.6 fusion.8
  284.7 4.9 all-to-all-start.6
  291.2 6.2 %multiply_reduce_fusion.2 = (f32[1024]{0:T(1024)S(1)}, f32[256]{0:T(256)S(1)}, f32[256,1024]{1,0:T(8,128)}) fusion(f32[256,1024]{1,0:T(8,128)S(1)} %copy-done.14, f32[256]{0:T(256)S(1)} %get-tuple-element.80, f32[1024]{0:T(1024)S(1)} %bitcast.370, bf16[256,3072]{0,1:T(8,128)(2,1)} %bitcast.326, bf16[1024,3072]{1,0:T(8,128)(2,1)} %param.16), kind=kOutput, calls=%fused_computation.113 | convolution fusion | flops 1612184320 | bytes 9971712 | tf_op jit(solution)/shard_map/dot_general | solution.py:72
  299.3 4.6 all-to-all-start.7
  306.9 3.1 fusion.9
  312.5 2.7 fusion.11
  315.2 8.4 %all-to-all-done.7 = bf16[8,32,1408]{2,1,0:T(8,128)(2,1)} async-done(((bf16[8,32,1408]{2,1,0:T(8,128)(2,1)}), bf16[8,32,1408]{2,1,0:T(8,128)(2,1)}, u32[]{:S(2)}, u32[]{:S(2)}) %all-to-all-start.7) | async-done | bytes 720928 | tf_op jit(solution)/shard_map/all_to_all | solution.py:289
  323.6 3.5 all-to-all-start.8
  333.4 3.1 fusion.29
  336.5 10.2 %all-to-all-done.8 = bf16[8,32,1408]{2,1,0:T(8,128)(2,1)S(1)} async-done(((bf16[8,32,1408]{2,1,0:T(8,128)(2,1)}), bf16[8,32,1408]{2,1,0:T(8,128)(2,1)S(1)}, u32[]{:S(2)}, u32[]{:S(2)}) %all-to-all-start.8) | async-done | bytes 720928 | tf_op jit(solution)/shard_map/all_to_all | solution.py:289
  346.6 3.8 all-to-all-start.9
  350.5 6.9 %collective-permute-done.2 = bf16[2,512,512]{2,1,0:T(8,128)(2,1)} collective-permute-done((bf16[2,512,512]{2,1,0:T(8,128)(2,1)}, bf16[2,512,512]{2,1,0:T(8,128)(2,1)}, u32[]{:S(2)}, u32[]{:S(2)}) %collective-permute-start.2) | collective-permute-done | bytes 1048608 | tf_op jit(solution)/shard_map/ppermute | solution.py:241
  360.4 6.1 %collective-permute-done.6 = bf16[2,256,1536]{2,1,0:T(8,128)(2,1)} collective-permute-done((bf16[2,256,1536]{2,1,0:T(8,128)(2,1)S(1)}, bf16[2,256,1536]{2,1,0:T(8,128)(2,1)}, u32[]{:S(2)}, u32[]{:S(2)}) %collective-permute-start.6) | collective-permute-done | bytes 1572896 | tf_op jit(solution)/shard_map/ppermute | solution.py:241
  366.6 2.9 fusion.16
  371.0 6.1 %collective-permute-done.3 = bf16[1,512,512]{2,1,0:T(8,128)(2,1)S(1)} collective-permute-done((bf16[1,512,512]{2,1,0:T(8,128)(2,1)S(1)}, bf16[1,512,512]{2,1,0:T(8,128)(2,1)S(1)}, u32[]{:S(2)}, u32[]{:S(2)}) %collective-permute-start.3) | collective-permute-done | bytes 524320 | tf_op jit(solution)/shard_map/ppermute | solution.py:241
  377.2 2.5 fusion.40
  379.7 4.8 all-to-all-start.4
  384.4 3.9 collective-permute-done.7
  388.3 3.5 fusion.4
  391.8 7.9 %all-to-all-done.4 = bf16[8,64,512]{2,1,0:T(8,128)(2,1)S(1)} async-done(((bf16[8,64,512]{2,1,0:T(8,128)(2,1)}), bf16[8,64,512]{2,1,0:T(8,128)(2,1)S(1)}, u32[]{:S(2)}, u32[]{:S(2)}) %all-to-all-start.4) | async-done | bytes 524320 | tf_op jit(solution)/shard_map/all_to_all | solution.py:289
  400.6 3.5 all-to-all-start.5
  406.0 3.3 fusion.30
  409.3 3.3 fusion.33
  412.6 130.0 %reduce-scatter.4.cloned.1.call-done = f32[32,4]{1,0:T(8,128)} async-done(((f32[1024,4]{1,0:T(8,128)}), f32[32,4]{1,0:T(8,128)}) %reduce-scatter.4.cloned.1.call-update) | async-done | bytes 528
  (354 shorter events, 119.8 us)
Async XLA Ops:
  7.2 103.9 %copy-start = (bf16[1024,1024]{1,0:T(8,128)(2,1)S(1)}, bf16[1024,1024]{1,0:T(8,128)(2,1)}, u32[]{:S(2)}) copy-start(bf16[1024,1024]{1,0:T(8,128)(2,1)} %param.17) | copy-start | bytes 6291460
  89.2 19.7 %all-to-all-start.1 = ((bf16[8,1,1,256,128]{4,3,2,1,0:T(8,128)(2,1)}), bf16[8,1,1,256,128]{4,3,2,1,0:T(8,128)(2,1)}, u32[]{:S(2)}, u32[]{:S(2)}) async-start(bf16[8,1,1,256,128]{4,3,2,1,0:T(8,128)(2,1)} %bitcast.15), calls=%async_computation.1 | async-start | bytes 1048576 | tf_op jit(solution)/shard_map/all_to_all | solution.py:321
  103.2 104.6 %collective-permute-start = (bf16[4,256,512]{1,2,0:T(8,128)(2,1)}, bf16[4,256,512]{1,2,0:T(8,128)(2,1)}, u32[]{:S(2)}, u32[]{:S(2)}) collective-permute-start(bf16[4,256,512]{1,2,0:T(8,128)(2,1)} %pad_maximum_fusion.10), channel_id=1, source_target_pairs={{0,4},{4,0},{8,12},{12,8},{16,20},{20,16},{24,28},{28,24},{1,5},{5... | collective-permute-start | bytes 3145736 | tf_op jit(solution)/shard_map/ppermute | solution.py:241
  108.4 93.6 %collective-permute-start.4 = (bf16[4,256,256]{1,2,0:T(8,128)(2,1)}, bf16[4,256,256]{1,2,0:T(8,128)(2,1)}, u32[]{:S(2)}, u32[]{:S(2)}) collective-permute-start(bf16[4,256,256]{1,2,0:T(8,128)(2,1)} %pad_maximum_fusion.16), channel_id=1, source_target_pairs={{0,4},{4,0},{8,12},{12,8},{16,20},{20,16},{24,28},{28,24},{1,5},{5... | collective-permute-start | bytes 1572872 | tf_op jit(solution)/shard_map/ppermute | solution.py:241
  139.6 8.9 %slice-start.2 = ((s8[5767168]{0:T(1024)(128)(4,1)}), s8[4194304]{0:T(1024)(128)(4,1)S(1)}, s32[]{:S(2)}) async-start(s8[5767168]{0:T(1024)(128)(4,1)} %bitcast.384), calls=%async_computation.14 | async-start | bytes 8388608
  140.8 7.7 %slice-start.3 = ((s8[5767168]{0:T(1024)(128)(4,1)}), s8[1572864]{0:T(1024)(128)(4,1)S(1)}, s32[]{:S(2)}) async-start(s8[5767168]{0:T(1024)(128)(4,1)} %bitcast.384), calls=%async_computation.15 | async-start | bytes 3145728
  155.9 20.0 %all-to-all-start.2 = ((bf16[8,1,1,256,128]{4,3,2,1,0:T(8,128)(2,1)}), bf16[8,1,1,256,128]{4,3,2,1,0:T(8,128)(2,1)S(1)}, u32[]{:S(2)}, u32[]{:S(2)}) async-start(bf16[8,1,1,256,128]{4,3,2,1,0:T(8,128)(2,1)} %copy.87), calls=%async_computation.2 | async-start | bytes 1048576 | tf_op jit(solution)/shard_map/all_to_all | solution.py:318
  160.9 4.9 collective-permute-start.8
  161.5 4.7 collective-permute-start.9
  162.3 6.3 %collective-permute-start.13 = (bf16[256,1408]{1,0:T(8,128)(2,1)S(1)}, bf16[256,1408]{1,0:T(8,128)(2,1)S(1)}, u32[]{:S(2)}, u32[]{:S(2)}) collective-permute-start(bf16[256,1408]{1,0:T(8,128)(2,1)S(1)} %get-tuple-element.44), channel_id=1, source_target_pairs={{0,4},{4,0},{8,12},{12,8},{16,20},{20,16},{24,28},{28,24},{1,5},{5... | collective-permute-start | bytes 2162696 | tf_op jit(solution)/shard_map/ppermute | solution.py:241
  165.8 2.5 collective-permute-start.12
  166.2 4.0 collective-permute-start.16
  168.3 25.8 %collective-permute-start.19 = (bf16[4,256,704]{1,2,0:T(8,128)(2,1)}, bf16[4,256,704]{1,2,0:T(8,128)(2,1)}, u32[]{:S(2)}, u32[]{:S(2)}) collective-permute-start(bf16[4,256,704]{1,2,0:T(8,128)(2,1)} %pad_maximum_fusion.8), channel_id=1, source_target_pairs={{0,4},{4,0},{8,12},{12,8},{16,20},{20,16},{24,28},{28,24},{1,5},{5... | collective-permute-start | bytes 4325384 | tf_op jit(solution)/shard_map/ppermute | solution.py:241
  168.7 27.5 %collective-permute-start.20 = (bf16[256,512]{1,0:T(8,128)(2,1)}, bf16[256,512]{1,0:T(8,128)(2,1)}, u32[]{:S(2)}, u32[]{:S(2)}) collective-permute-start(bf16[256,512]{1,0:T(8,128)(2,1)} %get-tuple-element.56), channel_id=1, source_target_pairs={{0,4},{4,0},{8,12},{12,8},{16,20},{20,16},{24,28},{28,24},{1,5},{5... | collective-permute-start | bytes 786440 | tf_op jit(solution)/shard_map/ppermute | solution.py:241
  170.2 34.8 %collective-permute-start.10 = (bf16[2,256,512]{2,1,0:T(8,128)(2,1)}, bf16[2,256,512]{2,1,0:T(8,128)(2,1)}, u32[]{:S(2)}, u32[]{:S(2)}) collective-permute-start(bf16[2,256,512]{2,1,0:T(8,128)(2,1)} %pad_maximum_fusion.19), channel_id=1, source_target_pairs={{0,2},{1,3},{2,0},{3,1},{4,6},{5,7},{6,4},{7,5},{8,10},{9,11},{10,... | collective-permute-start | bytes 1572872 | tf_op jit(solution)/shard_map/ppermute | solution.py:241
  189.1 95.6 %all-to-all-start.3 = ((bf16[8,1,3,256,128]{4,3,2,1,0:T(8,128)(2,1)}), bf16[8,1,3,256,128]{4,3,2,1,0:T(8,128)(2,1)S(1)}, u32[]{:S(2)}, u32[]{:S(2)}) async-start(bf16[8,1,3,256,128]{4,3,2,1,0:T(8,128)(2,1)} %attention_back.1), calls=%async_computation.3 | async-start | bytes 3145728 | tf_op jit(solution)/shard_map/all_to_all | solution.py:321
  194.1 34.4 %collective-permute-start.14 = (bf16[2,256,1408]{2,1,0:T(8,128)(2,1)}, bf16[2,256,1408]{2,1,0:T(8,128)(2,1)}, u32[]{:S(2)}, u32[]{:S(2)}) collective-permute-start(bf16[2,256,1408]{2,1,0:T(8,128)(2,1)} %pad_maximum_fusion.5), channel_id=1, source_target_pairs={{0,2},{1,3},{2,0},{3,1},{4,6},{5,7},{6,4},{7,5},{8,10},{9,11},{10,... | collective-permute-start | bytes 4325384 | tf_op jit(solution)/shard_map/ppermute | solution.py:241
  196.2 73.2 %collective-permute-start.17 = (bf16[2,256,1408]{2,1,0:T(8,128)(2,1)}, bf16[2,256,1408]{2,1,0:T(8,128)(2,1)}, u32[]{:S(2)}, u32[]{:S(2)}) collective-permute-start(bf16[2,256,1408]{2,1,0:T(8,128)(2,1)} %pad_maximum_fusion.7), channel_id=1, source_target_pairs={{0,1},{1,0},{2,3},{3,2},{4,5},{5,4},{6,7},{7,6},{8,9},{9,8},{10,11... | collective-permute-start | bytes 4325384 | tf_op jit(solution)/shard_map/ppermute | solution.py:241
  202.0 71.5 %collective-permute-start.21 = (bf16[2,704,512]{2,1,0:T(8,128)(2,1)}, bf16[2,704,512]{2,1,0:T(8,128)(2,1)}, u32[]{:S(2)}, u32[]{:S(2)}) collective-permute-start(bf16[2,704,512]{2,1,0:T(8,128)(2,1)} %pad_maximum_fusion.9), channel_id=1, source_target_pairs={{0,1},{1,0},{2,3},{3,2},{4,5},{5,4},{6,7},{7,6},{8,9},{9,8},{10,11... | collective-permute-start | bytes 4325384 | tf_op jit(solution)/shard_map/ppermute | solution.py:241
  206.4 22.1 %copy-start.60 = (bf16[4,512,256]{1,2,0:T(8,128)(2,1)S(1)}, bf16[4,512,256]{1,2,0:T(8,128)(2,1)}, u32[]{:S(2)}) copy-start(bf16[4,512,256]{1,2,0:T(8,128)(2,1)} %copy-done.59) | copy-start | bytes 3145732
  206.4 22.1 %copy-start.72 = (bf16[256,1408]{1,0:T(8,128)(2,1)S(1)}, bf16[256,1408]{1,0:T(8,128)(2,1)}, u32[]{:S(2)}) copy-start(bf16[256,1408]{1,0:T(8,128)(2,1)} %copy-done.71) | copy-start | bytes 2162692
  206.4 22.0 %copy-start.89 = (bf16[256,1408]{1,0:T(8,128)(2,1)S(1)}, bf16[256,1408]{1,0:T(8,128)(2,1)}, u32[]{:S(2)}) copy-start(bf16[256,1408]{1,0:T(8,128)(2,1)} %copy-done.88) | copy-start | bytes 2162692
  206.4 61.0 %collective-permute-start.11 = (bf16[1,256,512]{2,1,0:T(8,128)(2,1)S(1)}, bf16[1,256,512]{2,1,0:T(8,128)(2,1)S(1)}, u32[]{:S(2)}, u32[]{:S(2)}) collective-permute-start(bf16[1,256,512]{2,1,0:T(8,128)(2,1)S(1)} %fusion.55), channel_id=1, source_target_pairs={{0,1},{1,0},{2,3},{3,2},{4,5},{5,4},{6,7},{7,6},{8,9},{9,8},{10,11... | collective-permute-start | bytes 786440 | tf_op jit(solution)/shard_map/ppermute | solution.py:241
  210.6 56.8 %copy-start.91 = (bf16[256,512]{1,0:T(8,128)(2,1)S(1)}, bf16[256,512]{1,0:T(8,128)(2,1)}, u32[]{:S(2)}) copy-start(bf16[256,512]{1,0:T(8,128)(2,1)} %copy-done.90) | copy-start | bytes 786436
  230.2 39.2 %copy-start.69 = (bf16[256,1408]{1,0:T(8,128)(2,1)S(1)}, bf16[256,1408]{1,0:T(8,128)(2,1)}, u32[]{:S(2)}) copy-start(bf16[256,1408]{1,0:T(8,128)(2,1)} %copy-done.68) | copy-start | bytes 2162692
  230.2 39.2 %copy-start.86 = (bf16[256,1408]{1,0:T(8,128)(2,1)S(1)}, bf16[256,1408]{1,0:T(8,128)(2,1)}, u32[]{:S(2)}) copy-start(bf16[256,1408]{1,0:T(8,128)(2,1)} %copy-done.85) | copy-start | bytes 2162692
  230.2 51.9 %collective-permute-start.15 = (bf16[1,256,1408]{2,1,0:T(8,128)(2,1)S(1)}, bf16[1,256,1408]{2,1,0:T(8,128)(2,1)S(1)}, u32[]{:S(2)}, u32[]{:S(2)}) collective-permute-start(bf16[1,256,1408]{2,1,0:T(8,128)(2,1)S(1)} %fusion.18), channel_id=1, source_target_pairs={{0,1},{1,0},{2,3},{3,2},{4,5},{5,4},{6,7},{7,6},{8,9},{9,8},{10,11... | collective-permute-start | bytes 2162696 | tf_op jit(solution)/shard_map/ppermute | solution.py:241
  272.0 34.9 %collective-permute-start.18 = (bf16[1,256,1408]{2,1,0:T(8,128)(2,1)}, bf16[1,256,1408]{2,1,0:T(8,128)(2,1)}, u32[]{:S(2)}, u32[]{:S(2)}) collective-permute-start(bf16[1,256,1408]{2,1,0:T(8,128)(2,1)} %fusion.17), channel_id=1, source_target_pairs={{0,2},{1,3},{2,0},{3,1},{4,6},{5,7},{6,4},{7,5},{8,10},{9,11},{10,... | collective-permute-start | bytes 2162696 | tf_op jit(solution)/shard_map/ppermute | solution.py:241
  276.4 57.0 %collective-permute-start.22 = (bf16[1,704,512]{2,1,0:T(8,128)(2,1)}, bf16[1,704,512]{2,1,0:T(8,128)(2,1)}, u32[]{:S(2)}, u32[]{:S(2)}) collective-permute-start(bf16[1,704,512]{2,1,0:T(8,128)(2,1)} %fusion.44), channel_id=1, source_target_pairs={{0,2},{1,3},{2,0},{3,1},{4,6},{5,7},{6,4},{7,5},{8,10},{9,11},{10,... | collective-permute-start | bytes 2162696 | tf_op jit(solution)/shard_map/ppermute | solution.py:241
  284.7 14.6 %all-to-all-start.6 = ((bf16[8,32,512]{2,1,0:T(8,128)(2,1)}), bf16[8,32,512]{2,1,0:T(8,128)(2,1)S(1)}, u32[]{:S(2)}, u32[]{:S(2)}) async-start(bf16[8,32,512]{2,1,0:T(8,128)(2,1)} %bitcast.80), calls=%async_computation.6 | async-start | bytes 524288 | tf_op jit(solution)/shard_map/all_to_all | solution.py:289
  298.7 13.9 %collective-permute-start.5 = (bf16[256,1536]{0,1:T(8,128)(2,1)}, bf16[256,1536]{0,1:T(8,128)(2,1)}, u32[]{:S(2)}, u32[]{:S(2)}) collective-permute-start(bf16[256,1536]{0,1:T(8,128)(2,1)} %get-tuple-element.36), channel_id=1, source_target_pairs={{0,4},{4,0},{8,12},{12,8},{16,20},{20,16},{24,28},{28,24},{1,5},{5... | collective-permute-start | bytes 2359304 | tf_op jit(solution)/shard_map/ppermute | solution.py:241
  299.3 24.3 %all-to-all-start.7 = ((bf16[8,32,1408]{2,1,0:T(8,128)(2,1)}), bf16[8,32,1408]{2,1,0:T(8,128)(2,1)}, u32[]{:S(2)}, u32[]{:S(2)}) async-start(bf16[8,32,1408]{2,1,0:T(8,128)(2,1)} %bitcast.356), calls=%async_computation.7 | async-start | bytes 1441792 | tf_op jit(solution)/shard_map/all_to_all | solution.py:289
  306.4 3.6 collective-permute-start.1
  312.5 14.6 %copy-start.65 = (bf16[256,1536]{0,1:T(8,128)(2,1)S(1)}, bf16[256,1536]{0,1:T(8,128)(2,1)}, u32[]{:S(2)}) copy-start(bf16[256,1536]{0,1:T(8,128)(2,1)} %get-tuple-element.35) | copy-start | bytes 2359300
  323.6 23.0 %all-to-all-start.8 = ((bf16[8,32,1408]{2,1,0:T(8,128)(2,1)}), bf16[8,32,1408]{2,1,0:T(8,128)(2,1)S(1)}, u32[]{:S(2)}, u32[]{:S(2)}) async-start(bf16[8,32,1408]{2,1,0:T(8,128)(2,1)} %bitcast.357), calls=%async_computation.8 | async-start | bytes 1441792 | tf_op jit(solution)/shard_map/all_to_all | solution.py:289
  329.2 37.4 %collective-permute-start.6 = (bf16[2,256,1536]{2,1,0:T(8,128)(2,1)S(1)}, bf16[2,256,1536]{2,1,0:T(8,128)(2,1)}, u32[]{:S(2)}, u32[]{:S(2)}) collective-permute-start(bf16[2,256,1536]{2,1,0:T(8,128)(2,1)S(1)} %pad_maximum_fusion.3), channel_id=1, source_target_pairs={{0,2},{1,3},{2,0},{3,1},{4,6},{5,7},{6,4},{7,5},{8,10},{9,11},{10,... | collective-permute-start | bytes 4718600 | tf_op jit(solution)/shard_map/ppermute | solution.py:241
  331.9 25.5 %collective-permute-start.2 = (bf16[2,512,512]{2,1,0:T(8,128)(2,1)}, bf16[2,512,512]{2,1,0:T(8,128)(2,1)}, u32[]{:S(2)}, u32[]{:S(2)}) collective-permute-start(bf16[2,512,512]{2,1,0:T(8,128)(2,1)} %pad_maximum_fusion.11), channel_id=1, source_target_pairs={{0,1},{1,0},{2,3},{3,2},{4,5},{5,4},{6,7},{7,6},{8,9},{9,8},{10,11... | collective-permute-start | bytes 3145736 | tf_op jit(solution)/shard_map/ppermute | solution.py:241
  346.6 33.0 %all-to-all-start.9 = ((bf16[8,88,512]{2,1,0:T(8,128)(2,1)}), bf16[8,88,512]{2,1,0:T(8,128)(2,1)S(1)}, u32[]{:S(2)}, u32[]{:S(2)}) async-start(bf16[8,88,512]{2,1,0:T(8,128)(2,1)} %bitcast.358), calls=%async_computation.9 | async-start | bytes 1441792 | tf_op jit(solution)/shard_map/all_to_all | solution.py:289
  350.4 16.1 %copy-start.66 = (bf16[256,1536]{0,1:T(8,128)(2,1)S(1)}, bf16[256,1536]{0,1:T(8,128)(2,1)}, u32[]{:S(2)}) copy-start(bf16[256,1536]{0,1:T(8,128)(2,1)} %get-tuple-element.35) | copy-start | bytes 2359300
  359.1 18.0 %copy-start.83 = (bf16[256,512]{1,0:T(8,128)(2,1)S(1)}, bf16[256,512]{1,0:T(8,128)(2,1)}, u32[]{:S(2)}) copy-start(bf16[256,512]{1,0:T(8,128)(2,1)} %copy-done.82) | copy-start | bytes 786436
  359.1 18.0 %copy-start.93 = (bf16[256,512]{1,0:T(8,128)(2,1)S(1)}, bf16[256,512]{1,0:T(8,128)(2,1)}, u32[]{:S(2)}) copy-start(bf16[256,512]{1,0:T(8,128)(2,1)} %copy-done.92) | copy-start | bytes 786436
  359.2 18.0 %collective-permute-start.3 = (bf16[1,512,512]{2,1,0:T(8,128)(2,1)S(1)}, bf16[1,512,512]{2,1,0:T(8,128)(2,1)S(1)}, u32[]{:S(2)}, u32[]{:S(2)}) collective-permute-start(bf16[1,512,512]{2,1,0:T(8,128)(2,1)S(1)} %fusion.47), channel_id=1, source_target_pairs={{0,2},{1,3},{2,0},{3,1},{4,6},{5,7},{6,4},{7,5},{8,10},{9,11},{10,... | collective-permute-start | bytes 1572872 | tf_op jit(solution)/shard_map/ppermute | solution.py:241
  369.5 18.8 %collective-permute-start.7 = (bf16[1,256,1536]{2,1,0:T(8,128)(2,1)}, bf16[1,256,1536]{2,1,0:T(8,128)(2,1)}, u32[]{:S(2)}, u32[]{:S(2)}) collective-permute-start(bf16[1,256,1536]{2,1,0:T(8,128)(2,1)} %fusion.16), channel_id=1, source_target_pairs={{0,1},{1,0},{2,3},{3,2},{4,5},{5,4},{6,7},{7,6},{8,9},{9,8},{10,11... | collective-permute-start | bytes 2359304 | tf_op jit(solution)/shard_map/ppermute | solution.py:241
  379.7 12.2 %copy-start.28 = (bf16[8,88,512]{2,1,0:T(8,128)(2,1)}, bf16[8,88,512]{2,1,0:T(8,128)(2,1)S(1)}, u32[]{:S(2)}) copy-start(bf16[8,88,512]{2,1,0:T(8,128)(2,1)S(1)} %all-to-all-done.9) | copy-start | bytes 2162692
  379.7 20.1 %all-to-all-start.4 = ((bf16[8,64,512]{2,1,0:T(8,128)(2,1)}), bf16[8,64,512]{2,1,0:T(8,128)(2,1)S(1)}, u32[]{:S(2)}, u32[]{:S(2)}) async-start(bf16[8,64,512]{2,1,0:T(8,128)(2,1)} %bitcast.47), calls=%async_computation.4 | async-start | bytes 1048576 | tf_op jit(solution)/shard_map/all_to_all | solution.py:289
  391.8 14.1 %copy-start.40 = (bf16[256,1024]{1,0:T(8,128)(2,1)S(1)}, bf16[256,1024]{1,0:T(8,128)(2,1)}, u32[]{:S(2)}) copy-start(bf16[256,1024]{1,0:T(8,128)(2,1)} %copy-done.39) | copy-start | bytes 1572868
  400.6 149.2 %all-to-all-start.5 = ((bf16[8,32,1536]{2,1,0:T(8,128)(2,1)}), bf16[8,32,1536]{2,1,0:T(8,128)(2,1)S(1)}, u32[]{:S(2)}, u32[]{:S(2)}) async-start(bf16[8,32,1536]{2,1,0:T(8,128)(2,1)} %bitcast.355), calls=%async_computation.5 | async-start | bytes 1572864 | tf_op jit(solution)/shard_map/all_to_all | solution.py:289
  404.1 138.5 %reduce-scatter.4.cloned.1.call-start = ((), (), s32[]{:S(2)}) async-start(), calls=%async_computation.11 | async-start | bytes 540672
  (86 other events, 273.5 us)
Sparse Core Ops, SparseCore 0:
  407.2 135.3 reduce-scatter.3
